TPU v7x, 1024 devices: a whole 4x4x32 slice. The times are simulated.
1024 devices in a mesh: dp: 8 (over x, y_hi), tensor: 128 (over z, y_lo, core).
Axes of the slice: x: 4, y: 4 (y_hi: 2, y_lo: 2; y = y_hi * 2 + y_lo), z: 32, core: 2. Of those that a mesh axis runs over, the one named last changes fastest.
Arguments:
- context: bfloat16 [1024, 6144], P('dp', 'tensor'), may hold values from -6 to 6
- w_out: bfloat16 [18432, 6144], P('tensor'), may hold values from -0.3125 to 0.3125
- out_grad: bfloat16 [1024, 18432], P('dp', 'tensor'), may hold values from -6 to 6
Outputs:
- projected: bfloat16 [1024, 18432], P('dp', 'tensor')
- context_grad: bfloat16 [1024, 6144], P('dp', 'tensor')
- weight_grad: float32 [18432, 6144], P('tensor', 'dp')
All inputs are finite; a program needn't handle non-finite values.
Results may differ from a plain program's by a relative error of at most 0.0085.
Values may be sent and summed in bfloat16 or wider, within the bound.
A program may use at most 32 MiB of HBM per device.

v0:
```python
import jax
import jax.numpy as jnp
from jax import lax
from jax.sharding import PartitionSpec as P


def local(context, w_out, out_grad):
    row_count = context.shape[0]
    width_local = w_out.shape[0]
    head_width = w_out.shape[1]
    segment = lax.all_gather(context, "tensor", axis=1, tiled=True)
    running = lax.dot_general(
        segment, w_out, (((1,), (1,)), ((), ())), preferred_element_type=jnp.float32
    )
    running, gathered = (running, segment)
    projected = running.astype(jnp.bfloat16)
    reduced = lax.psum_scatter(
        lax.dot_general(
            w_out, out_grad, (((0,), (1,)), ((), ())), preferred_element_type=jnp.float32
        ),
        "tensor",
        scatter_dimension=0,
        tiled=True,
    )
    context_grad = reduced.T.astype(jnp.bfloat16)
    col_share = head_width // lax.axis_size("dp")
    pieces = lax.all_to_all(gathered, "dp", split_axis=1, concat_axis=0, tiled=True)
    grad_rows_all = lax.all_gather(out_grad, "dp", axis=0, tiled=True)
    replicas = lax.axis_size("dp")
    pieces = pieces.reshape(replicas, row_count, col_share)
    grad_rows_all = grad_rows_all.reshape(replicas, row_count, width_local)
    partial_value = jnp.einsum(
        "rtd,rtq->rdq", grad_rows_all, pieces, preferred_element_type=jnp.float32
    ).astype(jnp.bfloat16)
    weight_grad = jnp.sum(partial_value.astype(jnp.float32), axis=0)
    return (projected, context_grad, weight_grad)


def solution(mesh):
    placed = (P("dp", "tensor"), P("tensor", None), P("dp", "tensor"))
    return jax.shard_map(
        local,
        mesh=mesh,
        in_specs=placed,
        out_specs=(P("dp", "tensor"), P("dp", "tensor"), P("tensor", "dp")),
        check_vma=False,
    )
```

profile of v0, /device:TPU:16, one launch (start us, length us, event | category | flops | bytes accessed | tf_op | source)
XLA Modules:
  0.0 708.6 jit_solution(14608306070041302924)
XLA Ops:
  7.2 0.0 copy-start
  7.2 0.0 all-gather.2.cloned.1.call-start
  7.2 0.7 all-gather.2.cloned.1.call-update
  7.9 0.0 reduce-scatter.2.cloned.1.call-start
  8.0 0.7 copy-done
  8.6 3.5 fusion.3
  12.1 0.0 reduce-scatter.2.cloned.1.call-update
  12.2 241.0 %all-gather.2.cloned.1.call-done = bf16[128,6144]{0,1:T(8,128)(2,1)} async-done(((bf16[128,48]{0,1:T(8,128)(2,1)}), bf16[128,6144]{0,1:T(8,128)(2,1)}) %all-gather.2.cloned.1.call-update) | async-done | bytes 1572880 | tf_op jit(solution)/shard_map/all_gather | solution.py:11
  253.2 2.6 copy.6
  255.7 0.0 copy-start.2
  255.7 0.0 copy-start.1
  255.8 7.4 %all-to-all-start = ((bf16[128,8,768]{2,0,1:T(8,128)(2,1)}), bf16[128,8,768]{2,0,1:T(8,128)(2,1)}, u32[]{:S(2)}, u32[]{:S(2)}) async-start(bf16[128,8,768]{2,0,1:T(8,128)(2,1)} %copy.6), calls=%async_computation.1 | async-start | bytes 3145728 | tf_op jit(solution)/shard_map/all_to_all | solution.py:27
  263.1 0.0 copy-done.2
  263.1 43.9 %all_gather.7 = bf16[1024,144]{0,1:T(8,128)(2,1)} all-gather(bf16[128,144]{0,1:T(8,128)(2,1)S(1)} %copy-done.2), channel_id=1, replica_groups=mesh['dp'=8,'tensor'=128] {'dp'}, dimensions={0}, use_global_device_ids=true | all-gather | bytes 331776 | tf_op jit(solution)/shard_map/all_gather | solution.py:28
  307.0 0.0 copy-done.1
  307.0 1.2 convolution_convert_fusion
  308.2 0.0 all-to-all-done
  308.2 2.9 convert_reduce_fusion
  311.1 389.3 %reduce-scatter.2.cloned.1.call-done = f32[48,128]{1,0:T(8,128)} async-done(((f32[6144,128]{1,0:T(8,128)}), f32[48,128]{1,0:T(8,128)}) %reduce-scatter.2.cloned.1.call-update) | async-done | bytes 24592 | tf_op jit(solution)/shard_map/reduce_scatter | solution.py:17
  700.4 1.3 convert_bitcast_fusion
Async XLA Ops:
  7.2 1.5 copy-start
  7.2 246.0 %all-gather.2.cloned.1.call-start = ((), (), s32[]{:S(2)}) async-start(), calls=%async_computation.2 | async-start | bytes 1585152 | tf_op jit(solution)/shard_map/all_gather | solution.py:11
  7.9 692.5 %reduce-scatter.2.cloned.1.call-start = ((), (), s32[]{:S(2)}) async-start(), calls=%async_computation.3 | async-start | bytes 3170304 | tf_op jit(solution)/shard_map/reduce_scatter | solution.py:17
  255.7 7.4 %copy-start.2 = (bf16[128,144]{0,1:T(8,128)(2,1)S(1)}, bf16[128,144]{0,1:T(8,128)(2,1)}, u32[]{:S(2)}) copy-start(bf16[128,144]{0,1:T(8,128)(2,1)} %param.5) | copy-start | bytes 110596
  255.7 51.2 %copy-start.1 = (bf16[128,6144]{0,1:T(8,128)(2,1)S(1)}, bf16[128,6144]{0,1:T(8,128)(2,1)}, u32[]{:S(2)}) copy-start(bf16[128,6144]{0,1:T(8,128)(2,1)} %all-gather.2.cloned.1.call-done) | copy-start | bytes 4718596
  255.8 52.5 %all-to-all-start = ((bf16[128,8,768]{2,0,1:T(8,128)(2,1)}), bf16[128,8,768]{2,0,1:T(8,128)(2,1)}, u32[]{:S(2)}, u32[]{:S(2)}) async-start(bf16[128,8,768]{2,0,1:T(8,128)(2,1)} %copy.6), calls=%async_computation.1 | async-start | bytes 3145728 | tf_op jit(solution)/shard_map/all_to_all | solution.py:27
Sparse Core Ops, SparseCore 0:
  10.8 242.3 all-gather.1
  256.6 443.7 reduce-scatter.1
where the time goes:
time: 709 us
  waiting for transfers between devices  631 us (89%)
  blocking collectives  43.9 us (6%)
  between operations  14.1 us (2%)
  matrix products  7.64 us (1%)
  starting transfers between devices  7.46 us (1%)
    reduce_scatter x1, waiting for transfers between devices, local(): lax.psum_scatter(lax.dot_general(w_out, out_grad, (((0,), (1,)), ((), ())...  389 us
    all_gather x1, waiting for transfers between devices, local(): segment = lax.all_gather(context, 'tensor', axis=1, tiled=True)  241 us
    all_gather x1, blocking collectives, local(): grad_rows_all = lax.all_gather(out_grad, 'dp', axis=0, tiled=True)  43.9 us
  transfers between devices with their start and end apart: 3, of which 2 were waited for; matrix products, arithmetic and copies ran while one was open for 1% of the time, Pallas kernels for 0%

commit v1 on v0

v1 whole, which is shorter than its diff:
```python
import jax
import jax.numpy as jnp
from jax import lax
from jax.experimental import pallas as pl
from jax.experimental.pallas import tpu as pltpu
from jax.sharding import PartitionSpec as P

MESH = pl.DeviceIdType.MESH
F32, BF16 = jnp.float32, jnp.bfloat16
R, G, Q, S, FB, TOK, ROWS = 8, 8, 4, 4, 48, 128, 144


def dot_nt(a, b):
    return lax.dot_general(a, b, (((1,), (1,)), ((), ())), preferred_element_type=F32)


def eye(n):
    return (
        lax.broadcasted_iota(jnp.int32, (n, n), 0) == lax.broadcasted_iota(jnp.int32, (n, n), 1)
    ).astype(F32).astype(BF16)


def kernel(
    ctx, w, og, proj, cg, wg,
    xt, pf, pc, rc, ysend, yrecv, nsend, nrecv, fsend, frecv, oga, x2,
    fa_s, fa_r, na_s, na_r, ya_s, ya_r, ca_s, ca_r, cb_s, cb_r, og_s, og_r, x_s, x_r, xc_s, xc_r,
    rc_s, rc_r, ry_s, ry_r, rn_s, rn_r, rf_s, rf_r,
):
    r = lax.axis_index("dp")
    t = lax.axis_index("tensor")
    z, s = t // 4, t % 4
    yl, c = s // 2, s % 2
    q, g = z % 4, z // 4
    sib = 2 * yl + (1 - c)
    par = 2 * (1 - yl) + c

    def at_z(d):
        return (r, ((z + d + 32) % 32) * 4 + s)

    core_dev, y_dev = (r, z * 4 + sib), (r, z * 4 + par)

    def rep(k, sp):
        return ((r + k) % R, z * 4 + sp)

    barrier = pltpu.get_barrier_semaphore()
    partners = [at_z(4 * k) for k in range(1, G)] + [at_z(d) for d in (1, -1, 2, -2)] + [core_dev, y_dev]
    partners += [rep(k, sp) for k in range(1, R) for sp in (s, par)]
    for device in partners:
        pl.semaphore_signal(barrier, inc=1, device_id=device, device_id_type=MESH)

    xt[g, q, s] = dot_nt(eye(FB), ctx[...]).astype(BF16)
    oga[r] = dot_nt(eye(ROWS), og[...]).astype(BF16)

    for j in range(16):
        part = jnp.dot(og[...], w[:, j * 384 : (j + 1) * 384], preferred_element_type=F32)
        part = part.T.reshape(2, S, FB, TOK)
        for i in range(2):
            zz = 2 * j + i
            pf[zz % 4, zz // 4] = part[i]
    for cls in range(Q):
        for y in range(2):
            pc[cls, y] = pf[cls, :, 2 * y + 1 - c].astype(BF16)

    pl.semaphore_wait(barrier, len(partners))

    pending = []

    def send(src, dst, ssem, rsem, device):
        copy = pltpu.make_async_remote_copy(
            src_ref=src, dst_ref=dst, send_sem=ssem, recv_sem=rsem, device_id=device, device_id_type=MESH
        )
        copy.start()
        pending.append(copy)

    def arrived(dst, ssem, rsem):
        pltpu.make_async_remote_copy(
            src_ref=dst, dst_ref=dst, send_sem=ssem, recv_sem=rsem, device_id=core_dev, device_id_type=MESH
        ).wait_recv()

    for k in (4, 3, 5, 2, 6, 1, 7):
        block = xt.at[g, q, s]
        send(block, block, fa_s.at[k], fa_r.at[g], at_z(4 * k))
    order = [(q + 2) % 4, (q + 1) % 4, (q + 3) % 4, q]
    for i, cls in enumerate(order):
        send(pc.at[cls], rc.at[cls], rc_s.at[i], rc_r.at[i], core_dev)
    for k in range(1, R):
        send(oga.at[r], oga.at[r], og_s.at[k], og_r.at[r], rep(k, s))

    for i, cls in enumerate(order):
        arrived(rc.at[cls], rc_s.at[i], rc_r.at[i])
        ysend[cls] = (pf[cls, :, par] + rc[cls, 1 - yl].astype(F32)).astype(BF16)
        send(ysend.at[cls], yrecv.at[cls], ry_s.at[i], ry_r.at[i], y_dev)
    for i, cls in enumerate(order):
        arrived(yrecv.at[cls], ry_s.at[i], ry_r.at[i])
        total = pf[cls, :, s] + rc[cls, yl].astype(F32) + yrecv[cls].astype(F32)
        if i == 3:
            pf[cls, :, s] = total
        else:
            nsend[i] = total.astype(BF16)
            if i == 0:
                send(nsend.at[0, 0:4], nrecv.at[0, 0:4], rn_s.at[0], rn_r.at[0], at_z(2))
                send(nsend.at[0, 4:8], nrecv.at[0, 4:8], rn_s.at[1], rn_r.at[1], at_z(-2))
            else:
                send(nsend.at[i], nrecv.at[i], rn_s.at[i + 1], rn_r.at[i + 1], at_z(1 if i == 1 else -1))

    for k in range(1, G):
        gg = (g + k) % G
        arrived(xt.at[gg, q, s], fa_s.at[k], fa_r.at[gg])
    own, half0, half1 = xt.at[:, q, s], xt.at[0:4, q, s], xt.at[4:8, q, s]
    send(own, own, na_s.at[0], na_r.at[0], at_z(1))
    send(own, own, na_s.at[1], na_r.at[1], at_z(-1))
    send(half0, half0, na_s.at[2], na_r.at[2], at_z(2))
    send(half1, half1, na_s.at[3], na_r.at[3], at_z(-2))

    def spread(i, cls):
        mine = xt.at[:, cls, s]
        send(mine, mine, ya_s.at[i], ya_r.at[i], y_dev)
        send(mine, mine, ca_s.at[i], ca_r.at[i], core_dev)

    spread(0, q)

    arrived(nrecv.at[0, 0:4], rn_s.at[0], rn_r.at[0])
    arrived(nrecv.at[0, 4:8], rn_s.at[1], rn_r.at[1])
    arrived(nrecv.at[1], rn_s.at[2], rn_r.at[2])
    arrived(nrecv.at[2], rn_s.at[3], rn_r.at[3])
    window = pf[q, :, s] + nrecv[0].astype(F32) + nrecv[1].astype(F32) + nrecv[2].astype(F32)
    pf[q, :, s] = window
    fsend[...] = window.astype(BF16)
    for k in (4, 3, 5, 2, 6, 1, 7):
        gg = (g + k) % G
        send(fsend.at[gg], frecv.at[g], rf_s.at[k], rf_r.at[g], at_z(4 * k))

    arrived(xt.at[:, (q + 3) % 4, s], na_s.at[0], na_r.at[0])
    arrived(xt.at[:, (q + 1) % 4, s], na_s.at[1], na_r.at[1])
    arrived(xt.at[0:4, (q + 2) % 4, s], na_s.at[2], na_r.at[2])
    arrived(xt.at[4:8, (q + 2) % 4, s], na_s.at[3], na_r.at[3])
    for k in range(1, R):
        rr = (r + k) % R
        for j, sp in enumerate((s, par)):
            send(xt.at[rr, :, s], x2.at[r, :, s], x_s.at[k, j], x_r.at[r, yl], rep(k, sp))
    classes = [q, (q + 3) % 4, (q + 1) % 4, (q + 2) % 4]
    for i in range(1, Q):
        spread(i, classes[i])

    for k in range(1, R):
        gg = (r + k) % R
        arrived(oga.at[gg], og_s.at[k], og_r.at[gg])
    for i, cls in enumerate(classes):
        theirs = xt.at[:, cls, par]
        arrived(theirs, ya_s.at[i], ya_r.at[i])
        send(theirs, theirs, cb_s.at[i], cb_r.at[i], core_dev)

    for k in range(1, R):
        rr = (r + k) % R
        for y in range(2):
            piece = x2.at[rr, :, 2 * y + c]
            arrived(piece, x_s.at[k, y], x_r.at[rr, y])
            send(piece, piece, xc_s.at[k, y], xc_r.at[k, y], core_dev)

    for i, cls in enumerate(classes):
        arrived(xt.at[:, cls, sib], ca_s.at[i], ca_r.at[i])
        arrived(xt.at[:, cls, 2 * (1 - yl) + (1 - c)], cb_s.at[i], cb_r.at[i])
    total = jnp.zeros((ROWS, TOK), F32)
    for j in range(G):
        total += jnp.dot(
            w[:, j * 768 : (j + 1) * 768], xt[j].reshape(768, TOK), preferred_element_type=F32
        )
    proj[...] = dot_nt(eye(TOK), total.astype(BF16)).astype(BF16)
    x2[r] = xt[r]

    total = pf[q, g, s]
    for k in range(1, G):
        gg = (g + k) % G
        arrived(frecv.at[gg], rf_s.at[k], rf_r.at[gg])
        total += frecv[gg].astype(F32)
    cg[...] = dot_nt(eye(TOK), total.astype(BF16)).astype(BF16)

    for k in range(1, R):
        rr = (r + k) % R
        for y in range(2):
            arrived(x2.at[rr, :, 2 * y + 1 - c], xc_s.at[k, y], xc_r.at[k, y])
    grads = jnp.concatenate([oga[k] for k in range(R)], axis=1)
    for p in range(Q):
        columns = jnp.concatenate([x2[k, p].reshape(S * FB, TOK) for k in range(R)], axis=1)
        wg[:, p * S * FB : (p + 1) * S * FB] = dot_nt(grads, columns)

    for copy in pending:
        copy.wait_send()


def local(context, w_out, out_grad):
    vmem = pl.BlockSpec(memory_space=pltpu.VMEM)
    dma = pltpu.SemaphoreType.DMA
    return pl.pallas_call(
        kernel,
        out_shape=(
            jax.ShapeDtypeStruct((TOK, ROWS), BF16),
            jax.ShapeDtypeStruct((TOK, FB), BF16),
            jax.ShapeDtypeStruct((ROWS, Q * S * FB), F32),
        ),
        in_specs=[vmem] * 3,
        out_specs=(vmem,) * 3,
        scratch_shapes=[
            pltpu.VMEM((G, Q, S, FB, TOK), BF16),
            pltpu.VMEM((Q, G, S, FB, TOK), F32),
            pltpu.VMEM((Q, 2, G, FB, TOK), BF16),
            pltpu.VMEM((Q, 2, G, FB, TOK), BF16),
            pltpu.VMEM((Q, G, FB, TOK), BF16),
            pltpu.VMEM((Q, G, FB, TOK), BF16),
            pltpu.VMEM((3, G, FB, TOK), BF16),
            pltpu.VMEM((3, G, FB, TOK), BF16),
            pltpu.VMEM((G, FB, TOK), BF16),
            pltpu.VMEM((G, FB, TOK), BF16),
            pltpu.VMEM((R, ROWS, TOK), BF16),
            pltpu.VMEM((R, Q, S, FB, TOK), BF16),
            dma((G,)), dma((G,)), dma((4,)), dma((4,)), dma((Q,)), dma((Q,)), dma((Q,)), dma((Q,)),
            dma((Q,)), dma((Q,)), dma((R,)), dma((R,)), dma((R, 2)), dma((R, 2)), dma((R, 2)), dma((R, 2)),
            dma((Q,)), dma((Q,)), dma((Q,)), dma((Q,)), dma((4,)), dma((4,)), dma((G,)), dma((G,)),
        ],
        compiler_params=pltpu.CompilerParams(
            collective_id=0, has_side_effects=True, vmem_limit_bytes=40 * 2**20
        ),
        cost_estimate=pl.CostEstimate(
            flops=6 * TOK * ROWS * 6144, bytes_accessed=4_000_000, transcendentals=0
        ),
    )(context, w_out, out_grad)


def solution(mesh):
    placed = (P("dp", "tensor"), P("tensor", None), P("dp", "tensor"))
    return jax.shard_map(
        local,
        mesh=mesh,
        in_specs=placed,
        out_specs=(P("dp", "tensor"), P("dp", "tensor"), P("tensor", "dp")),
        check_vma=False,
    )
```

time: 709 us -> 77.3 us (0.11)
  the two profiles are of different devices: /device:TPU:16 before, /device:TPU:41 now
where the time goes in v1:
time: 77.3 us; the launch traced here: 77 us
  Pallas kernels  71.1 us (92%)
  local copies, waits for them, and re-layouts  5.33 us (7%)
    pallas_call x1, Pallas kernels, local(): pl.pallas_call(kernel, out_shape=(jax.ShapeDtypeStruct((TOK, ROWS), BF16)...  71.1 us
    unnamed x5, local copies, waits for them, and re-layouts  3.93 us

profile of v1, /device:TPU:41, one launch (start us, length us, event | category | flops | bytes accessed | tf_op | source)
XLA Modules:
  0.0 77.0 jit_solution(2240550691359963055)
XLA Ops:
  0.6 0.8 %copy.6.ctx = bf16[128,48]{1,0:T(8,128)(2,1)S(1)} copy(bf16[128,48]{0,1:T(8,128)(2,1)} %param.3) | data formatting | bytes 24576 | tf_op args[0]
  1.4 0.9 %copy.7.og = bf16[128,144]{1,0:T(8,128)(2,1)S(1)} copy(bf16[128,144]{0,1:T(8,128)(2,1)} %param.5) | data formatting | bytes 73728 | tf_op args[2]
  2.3 0.0 copy-start
  2.3 1.5 %copy-done = bf16[144,6144]{1,0:T(8,128)(2,1)S(1)} copy-done((bf16[144,6144]{1,0:T(8,128)(2,1)S(1)}, bf16[144,6144]{1,0:T(8,128)(2,1)}, u32[]{:S(2)}) %copy-start) | copy-done | bytes 1769496
  3.8 71.1 %shard_map.58 = (bf16[128,144]{1,0:T(8,128)(2,1)S(1)}, bf16[128,48]{1,0:T(8,128)(2,1)S(1)}, f32[144,768]{1,0:T(8,128)S(1)}) custom-call(bf16[128,48]{1,0:T(8,128)(2,1)S(1)} %copy.6.ctx, bf16[144,6144]{1,0:T(8,128)(2,1)S(1)} %copy-done, bf16[128,144]{1,0:T(8,128)(2,1)S(1)} %copy.7.og), custom_call_target="tpu_custom_call" | custom-call | flops 679477248 | bytes 4000000 | tf_op jit(solution)/shard_map/pallas_call | solution.py:194
  74.9 0.7 copy.8
  75.6 0.7 copy.9
  76.3 0.8 copy.11
Async XLA Ops:
  2.3 1.5 %copy-start = (bf16[144,6144]{1,0:T(8,128)(2,1)S(1)}, bf16[144,6144]{1,0:T(8,128)(2,1)}, u32[]{:S(2)}) copy-start(bf16[144,6144]{1,0:T(8,128)(2,1)} %w.1) | copy-start | bytes 5308420

commit v2 on v0

v2 whole, which is shorter than its diff:
```python
import jax
import jax.numpy as jnp
from jax import lax
from jax.experimental import pallas as pl
from jax.experimental.pallas import tpu as pltpu
from jax.sharding import PartitionSpec as P

MESH = pl.DeviceIdType.MESH
F32, BF16 = jnp.float32, jnp.bfloat16
R, G, Q, S, FB, TOK, ROWS = 8, 8, 4, 4, 48, 128, 144


def dot_nt(a, b):
    return lax.dot_general(a, b, (((1,), (1,)), ((), ())), preferred_element_type=F32)


def eye(n):
    return (
        lax.broadcasted_iota(jnp.int32, (n, n), 0) == lax.broadcasted_iota(jnp.int32, (n, n), 1)
    ).astype(F32).astype(BF16)


def kernel(
    ctx, w, og, proj, cg, wg,
    xt, wv, pf, pc, rc, ysend, yrecv, nsend, nrecv, fsend, frecv, oga, x2, own_ctx, cg_half,
    ok, in_s, a_s, ns_s, x_s, b_s, xf_s, rc_s, ry_s, rn_s, rf_s, fa_s, og_s, one_s,
    fa_r, na_r, ya_r, ca_r, cb_r, og_r, x_r, xf_r, rc_r, ry_r, rn_r, rf_r, cx_r, cg_r,
):
    r = lax.axis_index("dp")
    t = lax.axis_index("tensor")
    z, s = t // 4, t % 4
    yl, c = s // 2, s % 2
    q, g = z % 4, z // 4
    sib = 2 * yl + (1 - c)
    par = 2 * (1 - yl) + c

    def at(gp, qp):
        return (r, (4 * gp + qp) * 4 + s)

    def at_z(zz):
        return (r, zz * 4 + s)

    near = [(q + d) % 4 for d in range(4)]
    core_dev, y_dev = (r, z * 4 + sib), (r, z * 4 + par)

    loads = [
        pltpu.make_async_copy(og, oga.at[r], in_s.at[0]),
        pltpu.make_async_copy(w, wv, in_s.at[1]),
        pltpu.make_async_copy(ctx, own_ctx, in_s.at[2]),
    ]
    for load in loads:
        load.start()

    def greet(semaphore, device):
        pl.semaphore_signal(semaphore, inc=1, device_id=device, device_id_type=MESH)

    rank = jnp.where(g < 4, g, 11 - g)

    def above(gp):
        return (gp if gp < 4 else 11 - gp) > rank

    def below(gp):
        return (gp if gp < 4 else 11 - gp) < rank

    def beside(gp):
        return ((gp - g + 8) % 8 == 1) | ((gp - g + 8) % 8 == 7)

    def meets(gp):
        return beside(gp) | ((c == 0) & ((g < 4) != (gp < 4)))

    def number(condition):
        return jnp.where(condition, 1, 0)

    ends = (z == 0) | (z == 3) | (z == 28) | (z == 31)
    facing = jnp.where((z == 0) | (z == 28), z + 3, jnp.where(ends, z - 3, z))
    expected = number(ends)
    barrier = pltpu.get_barrier_semaphore()
    for d in (1, -1, 2, -2):

        @pl.when((z + d >= 0) & (z + d < 32))
        def _():
            greet(barrier, at_z(z + d))

        expected += number((z + d >= 0) & (z + d < 32))

    @pl.when(ends)
    def _():
        greet(barrier, at_z(facing))

    partners = [core_dev, y_dev]
    for k in range(1, R):
        partners += [((r + k) % R, z * 4 + sp) for sp in ((s, par) if k % 2 else (s,))]
    for gp in range(G):

        @pl.when(above(gp) & meets(gp))
        def _():
            greet(barrier, at(gp, q))

        expected += number(below(gp) & meets(gp))
    for device in partners:
        greet(barrier, device)

    loads[0].wait()
    grad = dot_nt(eye(TOK), oga[r]).astype(BF16)
    loads[1].wait()
    for j in range(16):
        part = jnp.dot(grad, wv[:, j * 384 : (j + 1) * 384], preferred_element_type=F32)
        part = part.T.reshape(2, 2, 2, FB, TOK)
        for i in range(2):
            zz = 2 * j + i
            pf[zz % 4, zz // 4] = part[i]
    order = (2, 1, 3, 0)

    @pl.when(c == 0)
    def _():
        for d in order:
            pc[near[d]] = pf[near[d]].astype(BF16)

    loads[2].wait()
    pl.semaphore_wait(barrier, len(partners) + expected)

    def copy_of(src, dst, ssem, rsem, device):
        return pltpu.make_async_remote_copy(
            src_ref=src, dst_ref=dst, send_sem=ssem, recv_sem=rsem, device_id=device, device_id_type=MESH
        )

    def send(src, dst, ssem, rsem, device):
        copy_of(src, dst, ssem, rsem, device).start()

    def arrived(dst, rsem):
        copy_of(dst, dst, rsem, rsem, core_dev).wait_recv()

    def sent(all_of_it, ssem):
        copy_of(all_of_it, all_of_it, ssem, ssem, core_dev).wait_send()

    def share_grads():
        for k in range(1, R):
            send(oga.at[r], oga.at[r], og_s, og_r, ((r + k) % R, t))

    def half(h):
        return pl.ds(4 * h, 4)

    def straight(b, gp):
        return (b >= 4) & (gp < 4)

    def hop(k, step, act):
        b, target = (g - step * k + 8) % 8, (g + step + 8) % 8
        block = xt.at[b, q, yl]

        @pl.when(jnp.logical_not(straight(b, target)))
        def _():
            act(copy_of(block, block, fa_s.at[k if step == 1 else 4 + k], fa_r.at[b], at(target, q)))

    def jump(gp, act):
        block = xt.at[g, q, yl]

        @pl.when(g >= 4)
        def _():
            act(copy_of(block, block, fa_s.at[7 + gp], fa_r.at[g], at(gp, q)))

    def start(copy):
        copy.start()

    def wait_sent(copy):
        copy.wait_send()

    def rounds(wanted):
        for k, step in ((1, 1), (1, -1), (2, 1), (2, -1), (3, 1), (3, -1), (4, 1)):
            b = (g - step * k + 8) % 8

            @pl.when(wanted(b))
            def _():
                arrived(xt.at[b, q, yl], fa_r.at[b])
                if k < (4 if step == 1 else 3):
                    hop(k, step, start)

    def spread(d, h):
        mine = xt.at[half(h), near[d], yl]
        send(mine, mine, a_s, ya_r.at[d, h], y_dev)

    def near_sends(h, act):
        own = xt.at[half(h), q, yl]
        way = 2 if h == 0 else -2
        for i, slot, when, target in (
            (0, 2, (z + way >= 0) & (z + way < 32), z + way),
            (1, 0, z < 31, z + 1),
            (2, 1, z > 0, z - 1),
            (3, 0, z == 3, z - 3),
            (4, 1, z == 28, z + 3),
            (5, 2, (z == 2) | (z == 3) if h == 0 else (z == 28) | (z == 29), z - way),
        ):

            @pl.when(when)
            def _():
                act(copy_of(own, own, ns_s.at[i, h], na_r.at[slot, h], at_z(target)))

    def far_done(h):
        near_sends(h, start)
        spread(0, h)

    def near_arrived(h):
        for d, slot in ((3, 0), (1, 1), (2, 2)):
            arrived(xt.at[half(h), near[d], yl], na_r.at[slot, h])
            spread(d, h)
        mine = xt.at[half(h), :, yl]
        send(mine, mine, b_s, ca_r.at[h], core_dev)

    def pair_arrived(d, h):
        arrived(xt.at[half(h), near[d], 1 - yl], ya_r.at[d, h])
        for rr in range(4 * h, 4 * h + 4):

            @pl.when(rr != r)
            def _():
                target = (rr, z * 4 + jnp.where((rr - r + 8) % 2 == 0, s, par))
                send(xt.at[rr, near[d]], x2.at[r, near[d]], x_s, x_r.at[r], target)

    def pair_done(h):
        for d in (3, 1, 2):
            pair_arrived(d, h)
        theirs = xt.at[half(h), :, 1 - yl]
        send(theirs, theirs, b_s, cb_r.at[h], core_dev)

    def project():
        total = jnp.zeros((ROWS, TOK), F32)
        for j in range(G):
            total += jnp.dot(
                wv[:, j * 768 : (j + 1) * 768], xt[j].reshape(768, TOK), preferred_element_type=F32
            )
        proj[...] = total.astype(BF16)
        x2[r] = xt[r]

    def weight_grads():
        grads = jnp.concatenate([oga[k] for k in range(R)], axis=1)
        for p in range(Q):
            columns = jnp.concatenate([x2[k, p].reshape(S * FB, TOK) for k in range(R)], axis=1)
            wg[:, p * S * FB : (p + 1) * S * FB] = dot_nt(grads, columns)

    @pl.when(c == 0)
    def _():
        xt[g, q, yl, 0] = own_ctx[...]

    def answer():
        for gp in range(G):

            @pl.when(below(gp) & beside(gp))
            def _():
                greet(ok.at[g], at(gp, q))

    def admitted(step):
        for gp in range(G):

            @pl.when(above(gp) & ((gp - g + 8) % 8 == step % 8))
            def _():
                pl.semaphore_wait(ok.at[gp], 1)

    @pl.when(c == 0)
    def _():
        answer()
        for i, d in enumerate(order):
            send(pc.at[near[d]], rc.at[near[d]], rc_s, rc_r.at[i], core_dev)
        arrived(xt.at[g, q, yl, 1], cx_r)
        for gp in range(4):
            jump(gp, start)

        def first_hop(step):
            admitted(step)
            hop(0, step, start)

        @pl.when(g == 0)
        def _():
            first_hop(1)

        first_hop(-1)

        @pl.when(g > 0)
        def _():
            first_hop(1)

        share_grads()

        @pl.when(g < 4)
        def _():
            rounds(lambda b: b < 4)
            far_done(0)
            rounds(lambda b: b >= 4)
            far_done(1)

        @pl.when(g >= 4)
        def _():
            rounds(lambda b: b != (g + 4) % 8)
            far_done(1)
            rounds(lambda b: b == (g + 4) % 8)
            far_done(0)

        pair_arrived(0, 0)
        near_arrived(0)
        pair_arrived(0, 1)
        near_arrived(1)
        pair_done(0)
        pair_done(1)
        for k in range(1, R):
            rr = (r + k) % R
            arrived(x2.at[rr], x_r.at[rr])
            send(x2.at[rr], x2.at[rr], xf_s, xf_r, core_dev)
        project()
        arrived(oga.at[0:7], og_r)
        weight_grads()
        arrived(cg_half, cg_r)
        cg[...] = cg_half[...]
        for k in range(4):
            hop(k, 1, wait_sent)
        for k in range(3):
            hop(k, -1, wait_sent)
        for gp in range(4):
            jump(gp, wait_sent)
        for h in range(2):
            near_sends(h, wait_sent)
        sent(x2.at[0:4], a_s)
        sent(x2.at[0:7], x_s)
        sent(x2, b_s)
        sent(x2.at[0:7], xf_s)
        sent(pc, rc_s)
        sent(oga.at[0:7], og_s)

    @pl.when(c == 1)
    def _():
        send(own_ctx, xt.at[g, q, yl, 1], one_s.at[0], cx_r, core_dev)
        answer()
        share_grads()
        for i, d in enumerate(order):
            cls = near[d]
            arrived(rc.at[cls], rc_r.at[i])
            ysend[cls] = (pf[cls, :, 1 - yl] + rc[cls, :, 1 - yl].astype(F32)).astype(BF16)
            send(ysend.at[cls], yrecv.at[cls], ry_s, ry_r.at[i], y_dev)
        for i, d in enumerate(order):
            cls = near[d]
            arrived(yrecv.at[cls], ry_r.at[i])
            total = pf[cls, :, yl] + rc[cls, :, yl].astype(F32) + yrecv[cls].astype(F32)
            if d == 0:
                pf[cls, :, yl] = total
            else:
                nsend[d - 1] = total.astype(BF16)
                if d == 2:
                    i0, i1 = jnp.where(z < 2, 4, 2), jnp.where(z > 29, 4, 2)
                    send(nsend.at[1, 0:4], nrecv.at[i0, 0:4], rn_s, rn_r.at[i0], at_z(jnp.where(z < 2, z + 2, z - 2)))
                    i2 = jnp.where(z > 29, 4, 5)
                    send(nsend.at[1, 4:8], nrecv.at[i1, 4:8], rn_s, rn_r.at[i2], at_z(jnp.where(z > 29, z - 2, z + 2)))
                elif d == 1:
                    i0 = jnp.where(z == 31, 3, 1)
                    send(nsend.at[0], nrecv.at[i0], rn_s, rn_r.at[i0], at_z(jnp.where(z == 31, z - 3, z + 1)))
                else:
                    i0 = jnp.where(z == 0, 3, 0)
                    send(nsend.at[2], nrecv.at[i0], rn_s, rn_r.at[i0], at_z(jnp.where(z == 0, z + 3, z - 1)))
        for here, ref, sem in (
            (z < 31, nrecv.at[0], 0),
            (z > 0, nrecv.at[1], 1),
            (z < 30, nrecv.at[2, 0:4], 2),
            (z > 1, nrecv.at[2, 4:8], 5),
        ):

            @pl.when(here)
            def _():
                arrived(ref, rn_r.at[sem])

            @pl.when(jnp.logical_not(here))
            def _():
                ref[...] = jnp.zeros(ref.shape, BF16)

        window = pf[q, :, yl] + nrecv[0].astype(F32) + nrecv[1].astype(F32) + nrecv[2].astype(F32)
        pf[q, :, yl] = window
        for here, ref, sem, low, high in (
            ((z == 3) | (z == 28), nrecv.at[3], 3, 0, 8),
            ((z == 2) | (z == 3), nrecv.at[4, 0:4], 4, 0, 4),
            ((z == 28) | (z == 29), nrecv.at[4, 4:8], 4, 4, 8),
        ):

            @pl.when(here)
            def _():
                arrived(ref, rn_r.at[sem])
                pf[q, low:high, yl] += ref[...].astype(F32)

        admitted(1)
        admitted(-1)
        for k, step in ((1, 1), (1, -1), (2, 1), (2, -1), (3, 1), (3, -1), (4, 1)):
            last = 4 if step == 1 else 3
            slot = k - 1 if step == 1 else 3 + k
            partial = pf[q, (g + step * (last + 1 - k) + 8) % 8, yl]
            if k > 1:
                arrived(frecv.at[slot - 1], rf_r.at[slot - 1])
                partial += frecv[slot - 1].astype(F32)
            fsend[slot] = partial.astype(BF16)
            send(fsend.at[slot], frecv.at[slot], rf_s, rf_r.at[slot], at((g + step + 8) % 8, q))
        total = pf[q, g, yl]
        for slot in (6, 3):
            arrived(frecv.at[slot], rf_r.at[slot])
            total += frecv[slot].astype(F32)
        total = total.astype(BF16)
        sent(own_ctx, one_s.at[0])
        cg_half[...] = total[0]
        send(cg_half, cg_half, one_s.at[1], cg_r, core_dev)
        cg[...] = total[1]
        for h in range(2):
            arrived(xt.at[half(h), :, yl], ca_r.at[h])
            arrived(xt.at[half(h), :, 1 - yl], cb_r.at[h])
        project()
        arrived(oga.at[0:7], og_r)
        arrived(x2.at[0:7], xf_r)
        weight_grads()
        sent(cg_half, one_s.at[1])
        sent(ysend, ry_s)
        sent(nsend, rn_s)
        sent(fsend, rf_s)
        sent(oga.at[0:7], og_s)


def local(context, w_out, out_grad):
    vmem = pl.BlockSpec(memory_space=pltpu.VMEM)
    dma = pltpu.SemaphoreType.DMA
    projected, context_grad, weight_grad = pl.pallas_call(
        kernel,
        out_shape=(
            jax.ShapeDtypeStruct((ROWS, TOK), BF16),
            jax.ShapeDtypeStruct((FB, TOK), BF16),
            jax.ShapeDtypeStruct((ROWS, Q * S * FB), F32),
        ),
        in_specs=[pl.BlockSpec(memory_space=pltpu.HBM)] * 3,
        out_specs=(vmem,) * 3,
        scratch_shapes=[
            pltpu.VMEM((G, Q, 2, 2, FB, TOK), BF16),
            pltpu.VMEM((ROWS, G * Q * S * FB), BF16),
            pltpu.VMEM((Q, G, 2, 2, FB, TOK), F32),
            pltpu.VMEM((Q, G, 2, 2, FB, TOK), BF16),
            pltpu.VMEM((Q, G, 2, 2, FB, TOK), BF16),
            pltpu.VMEM((Q, G, 2, FB, TOK), BF16),
            pltpu.VMEM((Q, G, 2, FB, TOK), BF16),
            pltpu.VMEM((3, G, 2, FB, TOK), BF16),
            pltpu.VMEM((5, G, 2, FB, TOK), BF16),
            pltpu.VMEM((7, 2, FB, TOK), BF16),
            pltpu.VMEM((7, 2, FB, TOK), BF16),
            pltpu.VMEM((R, ROWS, TOK), BF16),
            pltpu.VMEM((R, Q, 2, 2, FB, TOK), BF16),
            pltpu.VMEM((FB, TOK), BF16),
            pltpu.VMEM((FB, TOK), BF16),
            pltpu.SemaphoreType.REGULAR((G,)), dma((3,)),
            dma, dma((6, 2)), dma, dma, dma, dma, dma, dma, dma, dma((11,)), dma, dma((2,)),
            dma((G,)), dma((3, 2)), dma((Q, 2)), dma((2,)), dma((2,)), dma, dma((R,)), dma, dma((Q,)), dma((Q,)),
            dma((6,)), dma((7,)), dma, dma,
        ],
        compiler_params=pltpu.CompilerParams(
            collective_id=0, has_side_effects=True, vmem_limit_bytes=52 * 2**20
        ),
        cost_estimate=pl.CostEstimate(
            flops=6 * TOK * ROWS * 6144, bytes_accessed=4_000_000, transcendentals=0
        ),
    )(context.T, w_out, out_grad.T)
    return projected.T, context_grad.T, weight_grad


def solution(mesh):
    placed = (P("dp", "tensor"), P("tensor", None), P("dp", "tensor"))
    return jax.shard_map(
        local,
        mesh=mesh,
        in_specs=placed,
        out_specs=(P("dp", "tensor"), P("dp", "tensor"), P("tensor", "dp")),
        check_vma=False,
    )
```

time: 709 us -> 72.5 us (0.10)
  the two profiles are of different devices: /device:TPU:16 before, /device:TPU:5 now
where the time goes in v2:
time: 72.5 us; the launch traced here: 72.2 us
  Pallas kernels  68.1 us (94%)
  local copies, waits for them, and re-layouts  3.45 us (5%)
    pallas_call x1, Pallas kernels, local(): pl.pallas_call(kernel, out_shape=(jax.ShapeDtypeStruct((ROWS, TOK), BF16)...  68.1 us
    unnamed x7, local copies, waits for them, and re-layouts  3.45 us

profile of v2, /device:TPU:5, one launch (start us, length us, event | category | flops | bytes accessed | tf_op | source)
XLA Modules:
  0.0 72.2 jit_solution(14186925356927991663)
XLA Ops:
  0.6 0.0 copy-start
  0.6 0.8 %copy-done = bf16[128,144]{0,1:T(8,128)(2,1)S(1)} copy-done((bf16[128,144]{0,1:T(8,128)(2,1)S(1)}, bf16[128,144]{0,1:T(8,128)(2,1)}, u32[]{:S(2)}) %copy-start) | copy-done | bytes 36888
  1.4 0.0 copy-start.1
  1.4 0.7 copy-done.1
  2.1 68.1 %shard_map.58 = (bf16[144,128]{1,0:T(8,128)(2,1)S(1)}, bf16[48,128]{1,0:T(8,128)(2,1)S(1)}, f32[144,768]{1,0:T(8,128)S(1)}) custom-call(bf16[48,128]{1,0:T(8,128)(2,1)S(1)} %bitcast.7, bf16[144,6144]{1,0:T(8,128)(2,1)} %w.1, bf16[144,128]{1,0:T(8,128)(2,1)S(1)} %bitcast.6), custom_call_target="tpu_custom_call" | custom-call | flops 679477248 | bytes 4000000 | tf_op jit(solution)/shard_map/pallas_call | solution.py:419
  70.2 0.6 copy.9
  70.8 0.6 copy.10
  71.4 0.8 %copy.11 = f32[144,768]{1,0:T(8,128)} copy(f32[144,768]{1,0:T(8,128)S(1)} %get-tuple-element.14) | data formatting | bytes 884736
Async XLA Ops:
  0.6 0.8 %copy-start = (bf16[128,144]{0,1:T(8,128)(2,1)S(1)}, bf16[128,144]{0,1:T(8,128)(2,1)}, u32[]{:S(2)}) copy-start(bf16[128,144]{0,1:T(8,128)(2,1)} %param.5) | copy-start | bytes 110596
  1.4 0.7 copy-start.1

commit v3 on v2

--- a/solution.py
+++ b/solution.py
@@ -33,6 +33,7 @@
     q, g = z % 4, z // 4
     sib = 2 * yl + (1 - c)
     par = 2 * (1 - yl) + c
+    oth = 2 * (1 - yl) + (1 - c)
 
     def at(gp, qp):
         return (r, (4 * gp + qp) * 4 + s)
@@ -65,8 +66,11 @@
     def beside(gp):
         return ((gp - g + 8) % 8 == 1) | ((gp - g + 8) % 8 == 7)
 
+    def straight(b, gp):
+        return ((b >= 4) & (gp < 3)) | ((b == 3) & (gp == 0))
+
     def meets(gp):
-        return beside(gp) | ((c == 0) & ((g < 4) != (gp < 4)))
+        return beside(gp) | straight(g, gp) | straight(gp, g)
 
     def number(condition):
         return jnp.where(condition, 1, 0)
@@ -89,7 +93,7 @@
 
     partners = [core_dev, y_dev]
     for k in range(1, R):
-        partners += [((r + k) % R, z * 4 + sp) for sp in ((s, par) if k % 2 else (s,))]
+        partners += [((r + k) % R, z * 4 + sp) for sp in ((s, par, oth) if k % 2 else (s, sib))]
     for gp in range(G):
 
         @pl.when(above(gp) & meets(gp))
@@ -140,23 +144,24 @@
     def half(h):
         return pl.ds(4 * h, 4)
 
-    def straight(b, gp):
-        return (b >= 4) & (gp < 4)
-
     def hop(k, step, act):
         b, target = (g - step * k + 8) % 8, (g + step + 8) % 8
         block = xt.at[b, q, yl]
 
-        @pl.when(jnp.logical_not(straight(b, target)))
+        goes = jnp.logical_not(straight(b, target))
+        if k == 3:
+            goes = (b < 2) if step == 1 else ((b == 2) | (b == 3) | (b == 7))
+
+        @pl.when(goes)
         def _():
             act(copy_of(block, block, fa_s.at[k if step == 1 else 4 + k], fa_r.at[b], at(target, q)))
 
     def jump(gp, act):
         block = xt.at[g, q, yl]
 
-        @pl.when(g >= 4)
-        def _():
-            act(copy_of(block, block, fa_s.at[7 + gp], fa_r.at[g], at(gp, q)))
+        @pl.when(straight(g, gp))
+        def _():
+            act(copy_of(block, block, fa_s.at[8 + gp], fa_r.at[g], at(gp, q)))
 
     def start(copy):
         copy.start()
@@ -171,8 +176,10 @@
             @pl.when(wanted(b))
             def _():
                 arrived(xt.at[b, q, yl], fa_r.at[b])
-                if k < (4 if step == 1 else 3):
+                if k < 4:
                     hop(k, step, start)
+
+    held = ((0, 3), (1, 2))
 
     def spread(d, h):
         mine = xt.at[half(h), near[d], yl]
@@ -211,7 +218,8 @@
 
             @pl.when(rr != r)
             def _():
-                target = (rr, z * 4 + jnp.where((rr - r + 8) % 2 == 0, s, par))
+                ours, others = (s, par) if d in held[0] else (sib, oth)
+                target = (rr, z * 4 + jnp.where((rr - r + 8) % 2 == 0, ours, others))
                 send(xt.at[rr, near[d]], x2.at[r, near[d]], x_s, x_r.at[r], target)
 
     def pair_done(h):
@@ -219,6 +227,14 @@
             pair_arrived(d, h)
         theirs = xt.at[half(h), :, 1 - yl]
         send(theirs, theirs, b_s, cb_r.at[h], core_dev)
+
+    def exchange(mine):
+        for k in range(1, R):
+            rr = (r + k) % R
+            arrived(x2.at[rr, 0:2], x_r.at[rr])
+            for d in mine:
+                piece = x2.at[rr, near[d]]
+                send(piece, piece, xf_s, xf_r, core_dev)
 
     def project():
         total = jnp.zeros((ROWS, TOK), F32)
@@ -259,7 +275,7 @@
         for i, d in enumerate(order):
             send(pc.at[near[d]], rc.at[near[d]], rc_s, rc_r.at[i], core_dev)
         arrived(xt.at[g, q, yl, 1], cx_r)
-        for gp in range(4):
+        for gp in range(3):
             jump(gp, start)
 
         def first_hop(step):
@@ -298,29 +314,38 @@
         near_arrived(1)
         pair_done(0)
         pair_done(1)
-        for k in range(1, R):
-            rr = (r + k) % R
-            arrived(x2.at[rr], x_r.at[rr])
-            send(x2.at[rr], x2.at[rr], xf_s, xf_r, core_dev)
+        exchange(held[0])
         project()
         arrived(oga.at[0:7], og_r)
+        arrived(x2.at[0:7, 0:2], xf_r)
         weight_grads()
         arrived(cg_half, cg_r)
         cg[...] = cg_half[...]
         for k in range(4):
             hop(k, 1, wait_sent)
-        for k in range(3):
             hop(k, -1, wait_sent)
-        for gp in range(4):
+        for gp in range(3):
             jump(gp, wait_sent)
         for h in range(2):
             near_sends(h, wait_sent)
         sent(x2.at[0:4], a_s)
         sent(x2.at[0:7], x_s)
         sent(x2, b_s)
-        sent(x2.at[0:7], xf_s)
+        sent(x2.at[0:7, 0:2], xf_s)
         sent(pc, rc_s)
         sent(oga.at[0:7], og_s)
+
+    legs = ((1, 1), (1, -1), (2, 1), (2, -1), (3, 1), (3, -1), (4, 1))
+
+    def leg(k, step):
+        last = 4 if step == 1 else 3
+        target = (g + step * (last + 1 - k) + 8) % 8
+        goes = (target > 2) | (g < 4)
+        fed = (target > 2) | ((g - step >= 0) & (g - step < 4))
+        return (k - 1 if step == 1 else 3 + k), target, goes, fed
+
+    def rs_copy(slot, there, device):
+        return copy_of(fsend.at[slot], frecv.at[there], rf_s.at[slot], rf_r.at[there], device)
 
     @pl.when(c == 1)
     def _():
@@ -381,35 +406,77 @@
 
         admitted(1)
         admitted(-1)
-        for k, step in ((1, 1), (1, -1), (2, 1), (2, -1), (3, 1), (3, -1), (4, 1)):
-            last = 4 if step == 1 else 3
-            slot = k - 1 if step == 1 else 3 + k
-            partial = pf[q, (g + step * (last + 1 - k) + 8) % 8, yl]
+        for gp in range(3):
+
+            @pl.when(g >= 4)
+            def _():
+                fsend[7 + gp] = pf[q, gp, yl].astype(BF16)
+                rs_copy(7 + gp, 3 + g, at(gp, q)).start()
+
+        def pass_on(k, step, early):
+            slot, target, goes, fed = leg(k, step)
+            goes = goes & early(target)
+
+            @pl.when(goes)
+            def _():
+                fsend[slot] = pf[q, target, yl].astype(BF16)
+
             if k > 1:
-                arrived(frecv.at[slot - 1], rf_r.at[slot - 1])
-                partial += frecv[slot - 1].astype(F32)
-            fsend[slot] = partial.astype(BF16)
-            send(fsend.at[slot], frecv.at[slot], rf_s, rf_r.at[slot], at((g + step + 8) % 8, q))
-        total = pf[q, g, yl]
-        for slot in (6, 3):
-            arrived(frecv.at[slot], rf_r.at[slot])
-            total += frecv[slot].astype(F32)
-        total = total.astype(BF16)
+
+                @pl.when(goes & fed)
+                def _():
+                    arrived(frecv.at[slot - 1], rf_r.at[slot - 1])
+                    fsend[slot] = (pf[q, target, yl] + frecv[slot - 1].astype(F32)).astype(BF16)
+
+            @pl.when(goes)
+            def _():
+                rs_copy(slot, slot, at((g + step + 8) % 8, q)).start()
+
+        for k, step in legs[:2]:
+            pass_on(k, step, lambda target: target >= 0)
+        for k, step in legs[2:]:
+            pass_on(k, step, lambda target: target < 3)
+        for k, step in legs[2:]:
+            pass_on(k, step, lambda target: target >= 3)
+
+        for h in range(2):
+            arrived(xt.at[half(h), :, yl], ca_r.at[h])
+            arrived(xt.at[half(h), :, 1 - yl], cb_r.at[h])
+        project()
+        exchange(held[1])
+
+        for slot, here in [(6, g >= 0), (3, g != 0)] + [(b + 3, g < 3) for b in range(4, 8)]:
+
+            @pl.when(here)
+            def _():
+                arrived(frecv.at[slot], rf_r.at[slot])
+                pf[q, g, yl] += frecv[slot].astype(F32)
+
+        total = pf[q, g, yl].astype(BF16)
         sent(own_ctx, one_s.at[0])
         cg_half[...] = total[0]
         send(cg_half, cg_half, one_s.at[1], cg_r, core_dev)
         cg[...] = total[1]
-        for h in range(2):
-            arrived(xt.at[half(h), :, yl], ca_r.at[h])
-            arrived(xt.at[half(h), :, 1 - yl], cb_r.at[h])
-        project()
         arrived(oga.at[0:7], og_r)
-        arrived(x2.at[0:7], xf_r)
+        arrived(x2.at[0:7, 0:2], xf_r)
         weight_grads()
+        for gp in range(3):
+
+            @pl.when(g >= 4)
+            def _():
+                rs_copy(7 + gp, 3 + g, at(gp, q)).wait_send()
+
+        for k, step in legs:
+            slot, target, goes, fed = leg(k, step)
+
+            @pl.when(goes)
+            def _():
+                rs_copy(slot, slot, at((g + step + 8) % 8, q)).wait_send()
+
+        sent(x2.at[0:7, 0:2], xf_s)
         sent(cg_half, one_s.at[1])
         sent(ysend, ry_s)
         sent(nsend, rn_s)
-        sent(fsend, rf_s)
         sent(oga.at[0:7], og_s)
 
 
@@ -435,16 +502,16 @@
             pltpu.VMEM((Q, G, 2, FB, TOK), BF16),
             pltpu.VMEM((3, G, 2, FB, TOK), BF16),
             pltpu.VMEM((5, G, 2, FB, TOK), BF16),
-            pltpu.VMEM((7, 2, FB, TOK), BF16),
-            pltpu.VMEM((7, 2, FB, TOK), BF16),
+            pltpu.VMEM((10, 2, FB, TOK), BF16),
+            pltpu.VMEM((11, 2, FB, TOK), BF16),
             pltpu.VMEM((R, ROWS, TOK), BF16),
             pltpu.VMEM((R, Q, 2, 2, FB, TOK), BF16),
             pltpu.VMEM((FB, TOK), BF16),
             pltpu.VMEM((FB, TOK), BF16),
             pltpu.SemaphoreType.REGULAR((G,)), dma((3,)),
-            dma, dma((6, 2)), dma, dma, dma, dma, dma, dma, dma, dma((11,)), dma, dma((2,)),
+            dma, dma((6, 2)), dma, dma, dma, dma, dma, dma, dma((10,)), dma((11,)), dma, dma((2,)),
             dma((G,)), dma((3, 2)), dma((Q, 2)), dma((2,)), dma((2,)), dma, dma((R,)), dma, dma((Q,)), dma((Q,)),
-            dma((6,)), dma((7,)), dma, dma,
+            dma((6,)), dma((11,)), dma, dma,
         ],
         compiler_params=pltpu.CompilerParams(
             collective_id=0, has_side_effects=True, vmem_limit_bytes=52 * 2**20

time: 72.5 us -> 64.5 us (0.89)
  the two profiles are of different devices: /device:TPU:5 before, /device:TPU:966 now
where the time goes in v3:
time: 64.5 us; the launch traced here: 64.2 us
  Pallas kernels  60.1 us (93%)
  local copies, waits for them, and re-layouts  3.45 us (5%)
  between operations  0.65 us (1%)
    pallas_call x1, Pallas kernels, local(): pl.pallas_call(kernel, out_shape=(jax.ShapeDtypeStruct((ROWS, TOK), BF16)...  60.1 us
    unnamed x7, local copies, waits for them, and re-layouts  3.45 us

profile of v3, /device:TPU:966, one launch (start us, length us, event | category | flops | bytes accessed | tf_op | source)
XLA Modules:
  0.0 64.2 jit_solution(8087439697816110051)
XLA Ops:
  0.6 0.0 copy-start
  0.6 0.8 %copy-done = bf16[128,144]{0,1:T(8,128)(2,1)S(1)} copy-done((bf16[128,144]{0,1:T(8,128)(2,1)S(1)}, bf16[128,144]{0,1:T(8,128)(2,1)}, u32[]{:S(2)}) %copy-start) | copy-done | bytes 36888
  1.4 0.0 copy-start.1
  1.4 0.7 %copy-done.1 = bf16[128,48]{0,1:T(8,128)(2,1)S(1)} copy-done((bf16[128,48]{0,1:T(8,128)(2,1)S(1)}, bf16[128,48]{0,1:T(8,128)(2,1)}, u32[]{:S(2)}) %copy-start.1) | copy-done | bytes 12312
  2.1 60.1 %shard_map.58 = (bf16[144,128]{1,0:T(8,128)(2,1)S(1)}, bf16[48,128]{1,0:T(8,128)(2,1)S(1)}, f32[144,768]{1,0:T(8,128)S(1)}) custom-call(bf16[48,128]{1,0:T(8,128)(2,1)S(1)} %bitcast.7, bf16[144,6144]{1,0:T(8,128)(2,1)} %w.1, bf16[144,128]{1,0:T(8,128)(2,1)S(1)} %bitcast.6), custom_call_target="tpu_custom_call" | custom-call | flops 679477248 | bytes 4000000 | tf_op jit(solution)/shard_map/pallas_call | solution.py:486
  62.2 0.6 copy.9
  62.8 0.6 copy.10
  63.4 0.8 %copy.11 = f32[144,768]{1,0:T(8,128)} copy(f32[144,768]{1,0:T(8,128)S(1)} %get-tuple-element.14) | data formatting | bytes 884736
Async XLA Ops:
  0.6 0.8 %copy-start = (bf16[128,144]{0,1:T(8,128)(2,1)S(1)}, bf16[128,144]{0,1:T(8,128)(2,1)}, u32[]{:S(2)}) copy-start(bf16[128,144]{0,1:T(8,128)(2,1)} %param.5) | copy-start | bytes 110596
  1.4 0.7 %copy-start.1 = (bf16[128,48]{0,1:T(8,128)(2,1)S(1)}, bf16[128,48]{0,1:T(8,128)(2,1)}, u32[]{:S(2)}) copy-start(bf16[128,48]{0,1:T(8,128)(2,1)} %param.3) | copy-start | bytes 36868

commit v4 on v3

--- a/solution.py
+++ b/solution.py
@@ -22,9 +22,9 @@
 
 def kernel(
     ctx, w, og, proj, cg, wg,
-    xt, wv, pf, pc, rc, ysend, yrecv, nsend, nrecv, fsend, frecv, oga, x2, own_ctx, cg_half,
-    ok, in_s, a_s, ns_s, x_s, b_s, xf_s, rc_s, ry_s, rn_s, rf_s, fa_s, og_s, one_s,
-    fa_r, na_r, ya_r, ca_r, cb_r, og_r, x_r, xf_r, rc_r, ry_r, rn_r, rf_r, cx_r, cg_r,
+    xt, wv, pf, pc, rc, ysend, yrecv, nsend, nrecv, fsend, frecv, oga, x2, own_ctx, cg_half, ogx, wgp, wgx,
+    ok, in_s, a_s, ns_s, x_s, b_s, ox_s, wx_s, rc_s, ry_s, rn_s, rf_s, fa_s, og_s, one_s,
+    fa_r, na_r, ya_r, ca_r, cb_r, og_r, x_r, ox_r, wx_r, rc_r, ry_r, rn_r, rf_r, cx_r, cg_r,
 ):
     r = lax.axis_index("dp")
     t = lax.axis_index("tensor")
@@ -220,21 +220,14 @@
             def _():
                 ours, others = (s, par) if d in held[0] else (sib, oth)
                 target = (rr, z * 4 + jnp.where((rr - r + 8) % 2 == 0, ours, others))
-                send(xt.at[rr, near[d]], x2.at[r, near[d]], x_s, x_r.at[r], target)
+                place = held[0].index(d) if d in held[0] else held[1].index(d)
+                send(xt.at[rr, near[d]], x2.at[r, near[d]], x_s, x_r.at[r, place], target)
 
     def pair_done(h):
         for d in (3, 1, 2):
             pair_arrived(d, h)
         theirs = xt.at[half(h), :, 1 - yl]
         send(theirs, theirs, b_s, cb_r.at[h], core_dev)
-
-    def exchange(mine):
-        for k in range(1, R):
-            rr = (r + k) % R
-            arrived(x2.at[rr, 0:2], x_r.at[rr])
-            for d in mine:
-                piece = x2.at[rr, near[d]]
-                send(piece, piece, xf_s, xf_r, core_dev)
 
     def project():
         total = jnp.zeros((ROWS, TOK), F32)
@@ -245,11 +238,30 @@
         proj[...] = total.astype(BF16)
         x2[r] = xt[r]
 
-    def weight_grads():
-        grads = jnp.concatenate([oga[k] for k in range(R)], axis=1)
+    def swap_grads():
+        arrived(oga.at[0:7], og_r)
+        send(oga, ogx, ox_s, ox_r, core_dev)
+
+    def products(mine):
+        arrived(ogx, ox_r)
+        rows = jnp.concatenate(
+            [jnp.concatenate([grads[k] for k in range(R)], axis=1) for grads in (ogx, oga)], axis=0
+        )
+        for i, d in enumerate(mine):
+            p = near[d]
+            for k in range(1, R):
+                rr = (r + k) % R
+                arrived(x2.at[rr, p], x_r.at[rr, i])
+            columns = jnp.concatenate([x2[k, p].reshape(S * FB, TOK) for k in range(R)], axis=1)
+            both = dot_nt(rows, columns)
+            wgx[i] = both[:ROWS]
+            send(wgx.at[i], wgp.at[p], wx_s, wx_r, core_dev)
+            wgp[p] = both[ROWS:]
+
+    def collect():
+        arrived(wgp.at[0:2], wx_r)
         for p in range(Q):
-            columns = jnp.concatenate([x2[k, p].reshape(S * FB, TOK) for k in range(R)], axis=1)
-            wg[:, p * S * FB : (p + 1) * S * FB] = dot_nt(grads, columns)
+            wg[:, p * S * FB : (p + 1) * S * FB] = wgp[p]
 
     @pl.when(c == 0)
     def _():
@@ -314,13 +326,7 @@
         near_arrived(1)
         pair_done(0)
         pair_done(1)
-        exchange(held[0])
-        project()
-        arrived(oga.at[0:7], og_r)
-        arrived(x2.at[0:7, 0:2], xf_r)
-        weight_grads()
-        arrived(cg_half, cg_r)
-        cg[...] = cg_half[...]
+        swap_grads()
         for k in range(4):
             hop(k, 1, wait_sent)
             hop(k, -1, wait_sent)
@@ -328,24 +334,45 @@
             jump(gp, wait_sent)
         for h in range(2):
             near_sends(h, wait_sent)
-        sent(x2.at[0:4], a_s)
-        sent(x2.at[0:7], x_s)
-        sent(x2, b_s)
-        sent(x2.at[0:7, 0:2], xf_s)
         sent(pc, rc_s)
         sent(oga.at[0:7], og_s)
+        project()
+        sent(x2.at[0:4], a_s)
+        sent(x2, b_s)
+        sent(oga, ox_s)
+        products(held[0])
+        arrived(cg_half, cg_r)
+        cg[...] = cg_half[...]
+        collect()
+        sent(x2.at[0:7], x_s)
+        sent(wgx, wx_s)
 
     legs = ((1, 1), (1, -1), (2, 1), (2, -1), (3, 1), (3, -1), (4, 1))
 
     def leg(k, step):
         last = 4 if step == 1 else 3
         target = (g + step * (last + 1 - k) + 8) % 8
-        goes = (target > 2) | (g < 4)
-        fed = (target > 2) | ((g - step >= 0) & (g - step < 4))
+        whole = (target > 3) | ((target == 3) & (step == -1))
+        goes = whole | (g < 4)
+        fed = whole | ((g - step >= 0) & (g - step < 4))
         return (k - 1 if step == 1 else 3 + k), target, goes, fed
 
     def rs_copy(slot, there, device):
         return copy_of(fsend.at[slot], frecv.at[there], rf_s.at[slot], rf_r.at[there], device)
+
+    def owner_sum():
+        for slot, here in [(6, g >= 0), (3, g != 0)] + [(b + 3, g < 3) for b in range(4, 8)]:
+
+            @pl.when(here)
+            def _():
+                arrived(frecv.at[slot], rf_r.at[slot])
+                pf[q, g, yl] += frecv[slot].astype(F32)
+
+        total = pf[q, g, yl].astype(BF16)
+        sent(own_ctx, one_s.at[0])
+        cg_half[...] = total[0]
+        send(cg_half, cg_half, one_s.at[1], cg_r, core_dev)
+        cg[...] = total[1]
 
     @pl.when(c == 1)
     def _():
@@ -421,6 +448,13 @@
             def _():
                 fsend[slot] = pf[q, target, yl].astype(BF16)
 
+            if (k, step) == (1, -1):
+
+                @pl.when(goes & (g == 6))
+                def _():
+                    arrived(frecv.at[11], rf_r.at[11])
+                    fsend[slot] = (pf[q, target, yl] + frecv[11].astype(F32)).astype(BF16)
+
             if k > 1:
 
                 @pl.when(goes & fed)
@@ -433,33 +467,26 @@
                 rs_copy(slot, slot, at((g + step + 8) % 8, q)).start()
 
         for k, step in legs[:2]:
-            pass_on(k, step, lambda target: target >= 0)
+            pass_on(k, step, lambda target: target != 3)
+
+        @pl.when(g == 7)
+        def _():
+            fsend[10] = pf[q, 3, yl].astype(BF16)
+            rs_copy(10, 11, at(6, q)).start()
+
         for k, step in legs[2:]:
-            pass_on(k, step, lambda target: target < 3)
-        for k, step in legs[2:]:
-            pass_on(k, step, lambda target: target >= 3)
-
+            pass_on(k, step, lambda target: target != 3)
+        for k, step in legs:
+            pass_on(k, step, lambda target: target == 3)
+
+        swap_grads()
+        sent(ysend, ry_s)
+        sent(nsend, rn_s)
+        sent(oga.at[0:7], og_s)
         for h in range(2):
             arrived(xt.at[half(h), :, yl], ca_r.at[h])
             arrived(xt.at[half(h), :, 1 - yl], cb_r.at[h])
         project()
-        exchange(held[1])
-
-        for slot, here in [(6, g >= 0), (3, g != 0)] + [(b + 3, g < 3) for b in range(4, 8)]:
-
-            @pl.when(here)
-            def _():
-                arrived(frecv.at[slot], rf_r.at[slot])
-                pf[q, g, yl] += frecv[slot].astype(F32)
-
-        total = pf[q, g, yl].astype(BF16)
-        sent(own_ctx, one_s.at[0])
-        cg_half[...] = total[0]
-        send(cg_half, cg_half, one_s.at[1], cg_r, core_dev)
-        cg[...] = total[1]
-        arrived(oga.at[0:7], og_r)
-        arrived(x2.at[0:7, 0:2], xf_r)
-        weight_grads()
         for gp in range(3):
 
             @pl.when(g >= 4)
@@ -473,11 +500,24 @@
             def _():
                 rs_copy(slot, slot, at((g + step + 8) % 8, q)).wait_send()
 
-        sent(x2.at[0:7, 0:2], xf_s)
+        @pl.when(g == 7)
+        def _():
+            rs_copy(10, 11, at(6, q)).wait_send()
+
+        @pl.when(g >= 4)
+        def _():
+            owner_sum()
+
+        products(held[1])
+
+        @pl.when(g < 4)
+        def _():
+            owner_sum()
+
+        collect()
         sent(cg_half, one_s.at[1])
-        sent(ysend, ry_s)
-        sent(nsend, rn_s)
-        sent(oga.at[0:7], og_s)
+        sent(oga, ox_s)
+        sent(wgx, wx_s)
 
 
 def local(context, w_out, out_grad):
@@ -502,16 +542,19 @@
             pltpu.VMEM((Q, G, 2, FB, TOK), BF16),
             pltpu.VMEM((3, G, 2, FB, TOK), BF16),
             pltpu.VMEM((5, G, 2, FB, TOK), BF16),
-            pltpu.VMEM((10, 2, FB, TOK), BF16),
             pltpu.VMEM((11, 2, FB, TOK), BF16),
+            pltpu.VMEM((12, 2, FB, TOK), BF16),
             pltpu.VMEM((R, ROWS, TOK), BF16),
             pltpu.VMEM((R, Q, 2, 2, FB, TOK), BF16),
             pltpu.VMEM((FB, TOK), BF16),
             pltpu.VMEM((FB, TOK), BF16),
+            pltpu.VMEM((R, ROWS, TOK), BF16),
+            pltpu.VMEM((Q, ROWS, S * FB), F32),
+            pltpu.VMEM((2, ROWS, S * FB), F32),
             pltpu.SemaphoreType.REGULAR((G,)), dma((3,)),
-            dma, dma((6, 2)), dma, dma, dma, dma, dma, dma, dma((10,)), dma((11,)), dma, dma((2,)),
-            dma((G,)), dma((3, 2)), dma((Q, 2)), dma((2,)), dma((2,)), dma, dma((R,)), dma, dma((Q,)), dma((Q,)),
-            dma((6,)), dma((11,)), dma, dma,
+            dma, dma((6, 2)), dma, dma, dma, dma, dma, dma, dma, dma((11,)), dma((11,)), dma, dma((2,)),
+            dma((G,)), dma((3, 2)), dma((Q, 2)), dma((2,)), dma((2,)), dma, dma((R, 2)), dma, dma, dma((Q,)), dma((Q,)),
+            dma((6,)), dma((12,)), dma, dma,
         ],
         compiler_params=pltpu.CompilerParams(
             collective_id=0, has_side_effects=True, vmem_limit_bytes=52 * 2**20

time: 64.5 us -> 63.2 us (0.980)
  the two profiles are of different devices: /device:TPU:966 before, /device:TPU:983 now
where the time goes in v4:
time: 63.2 us; the launch traced here: 62.9 us
  Pallas kernels  58.8 us (93%)
  local copies, waits for them, and re-layouts  3.45 us (5%)
  between operations  0.65 us (1%)
    pallas_call x1, Pallas kernels, local(): pl.pallas_call(kernel, out_shape=(jax.ShapeDtypeStruct((ROWS, TOK), BF16)...  58.8 us
    unnamed x7, local copies, waits for them, and re-layouts  3.45 us

profile of v4, /device:TPU:983, one launch (start us, length us, event | category | flops | bytes accessed | tf_op | source)
XLA Modules:
  0.0 62.9 jit_solution(8904757173735902597)
XLA Ops:
  0.6 0.0 copy-start
  0.6 0.8 %copy-done = bf16[128,144]{0,1:T(8,128)(2,1)S(1)} copy-done((bf16[128,144]{0,1:T(8,128)(2,1)S(1)}, bf16[128,144]{0,1:T(8,128)(2,1)}, u32[]{:S(2)}) %copy-start) | copy-done | bytes 36888
  1.4 0.0 copy-start.1
  1.4 0.7 %copy-done.1 = bf16[128,48]{0,1:T(8,128)(2,1)S(1)} copy-done((bf16[128,48]{0,1:T(8,128)(2,1)S(1)}, bf16[128,48]{0,1:T(8,128)(2,1)}, u32[]{:S(2)}) %copy-start.1) | copy-done | bytes 12312
  2.1 58.8 %shard_map.58 = (bf16[144,128]{1,0:T(8,128)(2,1)S(1)}, bf16[48,128]{1,0:T(8,128)(2,1)S(1)}, f32[144,768]{1,0:T(8,128)S(1)}) custom-call(bf16[48,128]{1,0:T(8,128)(2,1)S(1)} %bitcast.7, bf16[144,6144]{1,0:T(8,128)(2,1)} %w.1, bf16[144,128]{1,0:T(8,128)(2,1)S(1)} %bitcast.6), custom_call_target="tpu_custom_call" | custom-call | flops 679477248 | bytes 4000000 | tf_op jit(solution)/shard_map/pallas_call | solution.py:526
  61.0 0.6 copy.9
  61.6 0.6 copy.10
  62.2 0.8 %copy.11 = f32[144,768]{1,0:T(8,128)} copy(f32[144,768]{1,0:T(8,128)S(1)} %get-tuple-element.14) | data formatting | bytes 884736
Async XLA Ops:
  0.6 0.8 %copy-start = (bf16[128,144]{0,1:T(8,128)(2,1)S(1)}, bf16[128,144]{0,1:T(8,128)(2,1)}, u32[]{:S(2)}) copy-start(bf16[128,144]{0,1:T(8,128)(2,1)} %param.5) | copy-start | bytes 110596
  1.4 0.7 %copy-start.1 = (bf16[128,48]{0,1:T(8,128)(2,1)S(1)}, bf16[128,48]{0,1:T(8,128)(2,1)}, u32[]{:S(2)}) copy-start(bf16[128,48]{0,1:T(8,128)(2,1)} %param.3) | copy-start | bytes 36868

commit v5 on v4

--- a/solution.py
+++ b/solution.py
@@ -21,7 +21,7 @@
 
 
 def kernel(
-    ctx, w, og, proj, cg, wg,
+    both, w, proj, cg, wg,
     xt, wv, pf, pc, rc, ysend, yrecv, nsend, nrecv, fsend, frecv, oga, x2, own_ctx, cg_half, ogx, wgp, wgx,
     ok, in_s, a_s, ns_s, x_s, b_s, ox_s, wx_s, rc_s, ry_s, rn_s, rf_s, fa_s, og_s, one_s,
     fa_r, na_r, ya_r, ca_r, cb_r, og_r, x_r, ox_r, wx_r, rc_r, ry_r, rn_r, rf_r, cx_r, cg_r,
@@ -45,9 +45,9 @@
     core_dev, y_dev = (r, z * 4 + sib), (r, z * 4 + par)
 
     loads = [
-        pltpu.make_async_copy(og, oga.at[r], in_s.at[0]),
+        pltpu.make_async_copy(both.at[0:ROWS], oga.at[r], in_s.at[0]),
         pltpu.make_async_copy(w, wv, in_s.at[1]),
-        pltpu.make_async_copy(ctx, own_ctx, in_s.at[2]),
+        pltpu.make_async_copy(both.at[ROWS : ROWS + FB], own_ctx, in_s.at[2]),
     ]
     for load in loads:
         load.start()
@@ -530,7 +530,7 @@
             jax.ShapeDtypeStruct((FB, TOK), BF16),
             jax.ShapeDtypeStruct((ROWS, Q * S * FB), F32),
         ),
-        in_specs=[pl.BlockSpec(memory_space=pltpu.HBM)] * 3,
+        in_specs=[pl.BlockSpec(memory_space=pltpu.HBM)] * 2,
         out_specs=(vmem,) * 3,
         scratch_shapes=[
             pltpu.VMEM((G, Q, 2, 2, FB, TOK), BF16),
@@ -562,7 +562,7 @@
         cost_estimate=pl.CostEstimate(
             flops=6 * TOK * ROWS * 6144, bytes_accessed=4_000_000, transcendentals=0
         ),
-    )(context.T, w_out, out_grad.T)
+    )(jnp.concatenate([out_grad.T, context.T], axis=0), w_out)
     return projected.T, context_grad.T, weight_grad
 
 

time: 63.2 us -> 62.5 us (0.989)
  local copies, waits for them, and re-layouts: 3.45 us -> 1.98 us
  other arithmetic: 0 us -> 0.79 us
    unnamed x7 -> x3, local copies, waits for them, and re-layouts: 3.45 us -> 1.98 us
    concatenate x0 -> x1, other arithmetic: none -> 0.79 us  [local(): jnp.concatenate([out_grad.T, context.T], axis=0)]
where the time goes in v5:
time: 62.5 us; the launch traced here: 62.3 us
  Pallas kernels  58.8 us (94%)
  local copies, waits for them, and re-layouts  1.98 us (3%)
  other arithmetic  0.79 us (1%)
  between operations  0.64 us (1%)
    pallas_call x1, Pallas kernels, local(): pl.pallas_call(kernel, out_shape=(jax.ShapeDtypeStruct((ROWS, TOK), BF16)...  58.8 us
    unnamed x3, local copies, waits for them, and re-layouts  1.98 us

profile of v5, /device:TPU:983, one launch (start us, length us, event | category | flops | bytes accessed | tf_op | source)
XLA Modules:
  0.0 62.3 jit_solution(8071996061774366864)
XLA Ops:
  0.6 0.8 %pad_maximum_fusion.both = bf16[192,128]{1,0:T(8,128)(2,1)S(1)} fusion(bf16[48,128]{1,0:T(8,128)(2,1)} %bitcast.7, bf16[144,128]{1,0:T(8,128)(2,1)} %bitcast.6), kind=kLoop, calls=%fused_computation | loop fusion | flops 98304 | bytes 98304 | tf_op jit(solution)/shard_map/concatenate | solution.py:565
  1.4 58.8 %shard_map.58 = (bf16[144,128]{1,0:T(8,128)(2,1)S(1)}, bf16[48,128]{1,0:T(8,128)(2,1)S(1)}, f32[144,768]{1,0:T(8,128)S(1)}) custom-call(bf16[192,128]{1,0:T(8,128)(2,1)S(1)} %pad_maximum_fusion.both, bf16[144,6144]{1,0:T(8,128)(2,1)} %w.1), custom_call_target="tpu_custom_call" | custom-call | flops 679477248 | bytes 4000000 | tf_op jit(solution)/shard_map/pallas_call | solution.py:526
  60.3 0.6 copy.9
  60.9 0.6 copy.10
  61.5 0.8 %copy.11 = f32[144,768]{1,0:T(8,128)} copy(f32[144,768]{1,0:T(8,128)S(1)} %get-tuple-element.14) | data formatting | bytes 884736

commit v6 on v5

--- a/solution.py
+++ b/solution.py
@@ -214,7 +214,8 @@
 
     def pair_arrived(d, h):
         arrived(xt.at[half(h), near[d], 1 - yl], ya_r.at[d, h])
-        for rr in range(4 * h, 4 * h + 4):
+        for k in range(4):
+            rr = 4 * h + (r + k + 1) % 4
 
             @pl.when(rr != r)
             def _():

time: 62.5 us -> 62.8 us (level)
  no operation moved by 1% of the time
where the time goes in v6:
time: 62.8 us; the launch traced here: 62.5 us
  Pallas kernels  59.1 us (94%)
  local copies, waits for them, and re-layouts  1.98 us (3%)
  other arithmetic  0.79 us (1%)
  between operations  0.64 us (1%)
    pallas_call x1, Pallas kernels, local(): pl.pallas_call(kernel, out_shape=(jax.ShapeDtypeStruct((ROWS, TOK), BF16)...  59.1 us
    unnamed x3, local copies, waits for them, and re-layouts  1.98 us

profile of v6, /device:TPU:983, one launch (start us, length us, event | category | flops | bytes accessed | tf_op | source)
XLA Modules:
  0.0 62.5 jit_solution(12886823988990066864)
XLA Ops:
  0.6 0.8 %pad_maximum_fusion.both = bf16[192,128]{1,0:T(8,128)(2,1)S(1)} fusion(bf16[48,128]{1,0:T(8,128)(2,1)} %bitcast.7, bf16[144,128]{1,0:T(8,128)(2,1)} %bitcast.6), kind=kLoop, calls=%fused_computation | loop fusion | flops 98304 | bytes 98304 | tf_op jit(solution)/shard_map/concatenate | solution.py:566
  1.4 59.1 %shard_map.58 = (bf16[144,128]{1,0:T(8,128)(2,1)S(1)}, bf16[48,128]{1,0:T(8,128)(2,1)S(1)}, f32[144,768]{1,0:T(8,128)S(1)}) custom-call(bf16[192,128]{1,0:T(8,128)(2,1)S(1)} %pad_maximum_fusion.both, bf16[144,6144]{1,0:T(8,128)(2,1)} %w.1), custom_call_target="tpu_custom_call" | custom-call | flops 679477248 | bytes 4000000 | tf_op jit(solution)/shard_map/pallas_call | solution.py:527
  60.5 0.6 copy.9
  61.2 0.6 copy.10
  61.8 0.8 %copy.11 = f32[144,768]{1,0:T(8,128)} copy(f32[144,768]{1,0:T(8,128)S(1)} %get-tuple-element.14) | data formatting | bytes 884736
